TPU v7x, 512 devices: a whole 4x4x16 slice. The times are simulated.
512 devices in a mesh: member: 8 (over y, x_hi), space: 64 (over x_lo, z, core).
Axes of the slice: x: 4 (x_hi: 2, x_lo: 2; x = x_hi * 2 + x_lo), y: 4, z: 16, core: 2. Of those that a mesh axis runs over, the one named last changes fastest.
Arguments:
- latent: bfloat16 [16, 4096, 1024], P('member', 'space'), may hold values from -6 to 6
- edge_weight: float32 [3, 32768], P(None, 'space'), may hold values from 0.1 to 1
- neighbours: int32 [3, 32768], P(None, 'space'), may hold values from 0 to 4095, as said below
- band_rows: int32 [64], P('space'), may hold values from 1 to 512, 24576 in all
- w_in: bfloat16 [1024, 1024], replicated, may hold values from -0.1875 to 0.1875
- w_out: bfloat16 [69, 1024], replicated, may hold values from -0.1875 to 0.1875
- target: float32 [69, 32768], P(None, 'space'), may hold values from -80 to 80
Outputs:
- score: float32 [], replicated
- grad_latent: bfloat16 [16, 4096, 1024], P('member', 'space')
- grad_w_out: float32 [69, 1024], P(None, 'space')
Inputs may be any that keep to these rules, and one draw needn't show every extreme that they name: `neighbours`: the node of an edge at grid slot g lies in latitude band g // 512 or one of the two bands beside it, node band b holding nodes b * 64 to (b + 1) * 64 - 1. Band b holds real grid points in its first band_rows[b] slots and padding after them; some band is full.
All inputs are finite; a program needn't handle non-finite values. No bound on the sum of `band_rows` on one device may be relied on, other than what follows from the above.
Results may differ from a plain program's by a relative error of at most 0.0075.
Values may be sent and summed in bfloat16 or wider, within the bound.
No kernel may reach another device: no remote copies, remote signals or barrier semaphores. Data moves between devices by JAX's collectives and lax.ppermute only.
A program may use at most 64 MiB of HBM per device.

v0:
```python
import jax
import jax.numpy as jnp
from jax import lax
from jax.sharding import PartitionSpec as P

epsilon = 1e-06


def extended_2(array, sides, width):
    for axis, dim in sides:
        size, length = (lax.axis_size(axis), array.shape[dim])
        up = [(i, (i + 1) % size) for i in range(size - 1)]
        down = [(j, i) for i, j in up]
        last = lax.slice_in_dim(array, length - width, length, axis=dim)
        first = lax.slice_in_dim(array, 0, width, axis=dim)
        before = lax.ppermute(last, axis, up)
        after = lax.ppermute(first, axis, down)
        array = jnp.concatenate([before, array, after], axis=dim)
    return array


def passed_along(array, axis, by):
    length = lax.axis_size(axis)
    pairs = [(i, i + by) for i in range(length) if 0 <= i + by < length]
    return lax.ppermute(array, axis, pairs)


def partials(everyone, target_rows, valid_rows):
    deviation = everyone - target_rows[None]
    target_sums = jnp.sum(valid_rows * deviation * deviation, axis=(1, 2))

    def against(member_field):
        spread = everyone - member_field[None]
        return jnp.sum(valid_rows * spread * spread, axis=(1, 2))

    pair_sums = lax.map(against, everyone)
    return (target_sums, pair_sums, jnp.sum(valid_rows))


def finish(target_sums, pair_sums, cell_count, variables):
    members = target_sums.shape[0]
    cells = variables * cell_count
    target_dist = jnp.sqrt(target_sums / cells + epsilon)
    pair_dist = jnp.sqrt(pair_sums / cells + epsilon)
    apart = 1.0 - jnp.eye(members, dtype=jnp.float32)
    pair_coef = apart / pair_dist
    score = jnp.mean(target_dist) - jnp.sum(apart * pair_dist) / (2.0 * members * (members - 1))
    return (score, pair_coef, target_dist)


def member_grads(chosen, everyone, coef_rows, dist_rows, target_rows, valid_rows):
    members = everyone.shape[0]
    others = jnp.sum(coef_rows[:, :, None, None] * everyone[None], axis=1)
    spread = jnp.sum(coef_rows, axis=1)[:, None, None] * chosen - others
    toward = (chosen - target_rows[None]) / (members * dist_rows[:, None, None])
    return (valid_rows * (toward - spread / (members * (members - 1)))).astype(jnp.bfloat16)


def per_device(latent, edge_weight, neighbours, band_rows, w_in, w_out, target):
    members_dev, nodes_dev, latent_width = latent.shape
    neigh_count, row_count = edge_weight.shape
    variables = w_out.shape[0]
    band_index = lax.axis_index("space")
    extended = extended_2(latent, (("space", 1),), nodes_dev)
    local_index = neighbours - (band_index - 1) * nodes_dev
    picked = jnp.take(extended, local_index.reshape(-1), axis=1).reshape(
        members_dev, neigh_count, row_count, latent_width
    )
    aggregated = edge_weight[0][None, :, None] * picked[:, 0].astype(jnp.float32)
    for neighbour in range(1, neigh_count):
        aggregated = aggregated + edge_weight[neighbour][None, :, None] * picked[
            :, neighbour
        ].astype(jnp.float32)
    latent_mix = aggregated.astype(jnp.bfloat16)
    preact = jnp.einsum("mgd,de->mge", latent_mix, w_in, preferred_element_type=jnp.float32)
    hidden = jax.nn.silu(preact).astype(jnp.bfloat16)
    fields = jnp.einsum("vd,mgd->mvg", w_out, hidden, preferred_element_type=jnp.float32).astype(
        jnp.bfloat16
    )
    valid_rows = (jnp.arange(row_count) < band_rows[0]).astype(jnp.float32)
    everyone = lax.all_gather(fields, "member", axis=0, tiled=True).astype(jnp.float32)
    target_sums, pair_sums, cell_count = partials(everyone, target, valid_rows)
    target_sums, pair_sums, cell_count = lax.psum((target_sums, pair_sums, cell_count), "space")
    score, pair_coef, target_dist = finish(target_sums, pair_sums, cell_count, variables)
    first_member = lax.axis_index("member") * members_dev
    coef_rows = lax.dynamic_slice_in_dim(pair_coef, first_member, members_dev, 0)
    dist_rows = lax.dynamic_slice_in_dim(target_dist, first_member, members_dev, 0)
    grad_fields = member_grads(
        fields.astype(jnp.float32), everyone, coef_rows, dist_rows, target, valid_rows
    )
    partial_weight = jnp.einsum(
        "mvg,mgd->vd", grad_fields, hidden, preferred_element_type=jnp.float32
    )
    summed = lax.psum(partial_weight, ("member", "space"))
    column_count = latent_width // lax.axis_size("space")
    grad_w_out = lax.dynamic_slice_in_dim(summed, band_index * column_count, column_count, 1)
    back = jnp.einsum("vd,mvg->mgd", w_out, grad_fields, preferred_element_type=jnp.float32)
    sigmoid_part = jax.nn.sigmoid(preact)
    grad_pre = (back * sigmoid_part * (1.0 + preact * (1.0 - sigmoid_part))).astype(jnp.bfloat16)
    grad_mixed = jnp.einsum("mge,de->mgd", grad_pre, w_in, preferred_element_type=jnp.float32)
    spread_terms = (edge_weight[None, :, :, None] * grad_mixed[:, None]).reshape(
        members_dev, -1, latent_width
    )
    flat_index = local_index.reshape(-1)
    collected = jax.vmap(
        lambda edge_terms: jax.ops.segment_sum(edge_terms, flat_index, num_segments=3 * nodes_dev)
    )(spread_terms)
    lower_rim = collected[:, :nodes_dev].astype(jnp.bfloat16)
    middle_rows = collected[:, nodes_dev : 2 * nodes_dev]
    upper_rim = collected[:, 2 * nodes_dev :].astype(jnp.bfloat16)
    from_above = passed_along(lower_rim, "space", -1)
    from_below = passed_along(upper_rim, "space", 1)
    grad_latent = (
        middle_rows + from_above.astype(jnp.float32) + from_below.astype(jnp.float32)
    ).astype(jnp.bfloat16)
    return (score, grad_latent, grad_w_out)


def solution(mesh):
    return jax.shard_map(
        per_device,
        mesh=mesh,
        in_specs=(
            P("member", "space", None),
            P(None, "space"),
            P(None, "space"),
            P("space"),
            P(),
            P(),
            P(None, "space"),
        ),
        out_specs=(P(), P("member", "space", None), P(None, "space")),
        check_vma=False,
    )
```

profile of v0, /device:TPU:4, one launch (start us, length us, event | category | flops | bytes accessed | tf_op | source)
XLA Modules:
  0.0 1032.3 jit_solution(2826235210925329485)
XLA Ops:
  13.2 2.4 collective-permute-done.1
  17.6 41.8 %gather_fusion = bf16[1536,2,1024]{2,1,0:T(2,128)(2,1)} fusion(bf16[2,192,1024]{2,0,1:T(2,128)(2,1)S(1)} %pad_maximum_fusion, s32[2048]{0:T(1024)S(1)} %pad_clamp_fusion), kind=kCustom, calls=%fused_computation | custom fusion | bytes 12589056 | tf_op jit(solution)/shard_map/jit(_take)/gather | solution.py:66
  59.5 6.4 copy_select_fusion
  65.9 4.7 multiply_convert_fusion.1
  75.0 67.4 %all-gather.2.cloned.1.call-done = bf16[16,69,512]{2,1,0:T(8,128)(2,1)} async-done(((bf16[2,69,512]{2,1,0:T(8,128)(2,1)}), bf16[16,69,512]{2,1,0:T(8,128)(2,1)}) %all-gather.2.cloned.1.call-update) | async-done | bytes 1130512 | tf_op jit(solution)/shard_map/all_gather | solution.py:81
  142.3 3.0 convert_element_type.76
  145.4 59.9 %while.11 = (s32[]{:T(128)}, f32[16,16]{1,0:T(8,128)S(1)}, f32[16,69,512]{2,1,0:T(8,128)}, s32[]{:T(128)}, s32[]{:T(128)}, /*index=5*/s32[]{:T(128)}) while((s32[]{:T(128)}, f32[16,16]{1,0:T(8,128)S(1)}, f32[16,69,512]{2,1,0:T(8,128)}, s32[]{:T(128)}, s32[]{:T(128)}, /*index=5*/s32[]{:T(128)}) %tuple.38), condition=%wide.region_7.8_spmd.clone, body=%wide.region_5.7_spmd.clone.sunk | while | flops 2262002 | bytes 2689297 | solution.py:36
  147.0 2.1 fusion.44
  150.8 2.1 fusion.44
  154.5 2.1 fusion.44
  176.9 2.1 fusion.44
  180.7 2.1 fusion.44
  184.4 2.1 fusion.44
  188.2 2.1 fusion.44
  191.9 2.1 fusion.44
  195.6 2.1 fusion.44
  206.7 112.9 %all-reduce = (f32[16]{0:T(128)S(1)}, f32[]{:T(128)}, f32[16,16]{1,0:T(8,128)S(1)}) all-reduce(f32[16]{0:T(128)S(1)} %fusion.7, f32[]{:T(128)} %fusion.30, f32[16,16]{1,0:T(8,128)S(1)} %get-tuple-element.25), channel_id=1, replica_groups=mesh['member'=8,'space'=64] {'space'}, use_global_device_ids=true, to_apply=%region_1.2 | all-reduce | flops 273 | bytes 2184 | tf_op jit(solution)/shard_map/psum | solution.py:83
  323.2 7.9 fusion.10
  331.1 5.4 copy.33
  336.5 10.1 bitcast_multiply_fusion
  348.2 211.3 %scatter_fusion = f32[2,192,1024]{2,0,1:T(2,128)} fusion(f32[2,192,1024]{2,0,1:T(2,128)} %broadcast_in_dim.23, s32[1536]{0:T(1024)S(1)} %reshape.87, f32[1536,2,1024]{2,1,0:T(2,128)} %bitcast.66), kind=kCustom, calls=%fused_computation.1 | custom fusion | flops 3145728 | bytes 37754880 | tf_op jit(solution)/shard_map/vmap()/scatter-add | solution.py:106
  563.8 3.0 collective-permute-start.3
  566.9 3.4 convolution_bitcast_fusion
  571.6 449.3 %all-reduce.3.cloned.1.call-done = f32[69,1024]{0,1:T(8,128)} async-done(((f32[69,1024]{0,1:T(8,128)}), f32[69,1024]{0,1:T(8,128)}) %all-reduce.3.cloned.1.call-update) | async-done | bytes 282640 | tf_op jit(solution)/shard_map/psum | solution.py:94
  (103 shorter events, 65.9 us)
Async XLA Ops:
  7.2 58.7 %copy-start = (bf16[1024,1024]{1,0:T(8,128)(2,1)S(1)}, bf16[1024,1024]{1,0:T(8,128)(2,1)}, u32[]{:S(2)}) copy-start(bf16[1024,1024]{1,0:T(8,128)(2,1)} %param.13) | copy-start | bytes 6291460
  7.2 135.2 %all-gather.2.cloned.1.call-start = ((), (), s32[]{:S(2)}) async-start(), calls=%async_computation | async-start | bytes 1327104 | tf_op jit(solution)/shard_map/all_gather | solution.py:81
  8.6 4.7 collective-permute-start
  10.4 5.3 collective-permute-start.1
  65.9 6.1 copy-start.4
  65.9 7.8 copy-start.5
  70.6 1.4 copy-start.2
  73.4 947.4 %all-reduce.3.cloned.1.call-start = ((), (), s32[]{:S(2)}) async-start(), calls=%async_computation.1 | async-start | bytes 1048576 | tf_op jit(solution)/shard_map/psum | solution.py:94
  145.4 59.9 %copy-start.1 = (bf16[16,69,512]{2,1,0:T(8,128)(2,1)S(1)}, bf16[16,69,512]{2,1,0:T(8,128)(2,1)}, u32[]{:S(2)}) copy-start(bf16[16,69,512]{2,1,0:T(8,128)(2,1)} %all-gather.2.cloned.1.call-done) | copy-start | bytes 3391492
  205.3 117.9 %copy-start.3 = (bf16[2,69,512]{2,1,0:T(8,128)(2,1)S(1)}, bf16[2,69,512]{2,1,0:T(8,128)(2,1)}, u32[]{:S(2)}) copy-start(bf16[2,69,512]{2,1,0:T(8,128)(2,1)} %fusion.16) | copy-start | bytes 423940
  562.5 459.7 %collective-permute-start.2 = (bf16[2,64,1024]{2,0,1:T(2,128)(2,1)}, bf16[2,64,1024]{2,0,1:T(2,128)(2,1)S(1)}, u32[]{:S(2)}, u32[]{:S(2)}) collective-permute-start(bf16[2,64,1024]{2,0,1:T(2,128)(2,1)} %get-tuple-element.68), channel_id=1, source_target_pairs={{1,0},{2,1},{3,2},{4,3},{5,4},{6,5},{7,6},{8,7},{9,8},{10,9},{11,1... | collective-permute-start | bytes 786440 | tf_op jit(solution)/shard_map/ppermute | solution.py:25
  563.8 458.4 %collective-permute-start.3 = (bf16[2,64,1024]{2,0,1:T(2,128)(2,1)S(1)}, bf16[2,64,1024]{2,0,1:T(2,128)(2,1)S(1)}, u32[]{:S(2)}, u32[]{:S(2)}) collective-permute-start(bf16[2,64,1024]{2,0,1:T(2,128)(2,1)S(1)} %get-tuple-element.69), channel_id=1, source_target_pairs={{0,1},{1,2},{2,3},{3,4},{4,5},{5,6},{6,7},{7,8},{8,9},{9,10},{10,1... | collective-permute-start | bytes 786440 | tf_op jit(solution)/shard_map/ppermute | solution.py:25
Sparse Core Ops, SparseCore 0:
  73.6 68.7 all-gather.1
  570.4 450.4 all-reduce.2
where the time goes:
time: 1040 us; the launch traced here: 1030 us
  waiting for transfers between devices  519 us (50%)
  other arithmetic  286 us (28%)
  blocking collectives  113 us (11%)
  local copies, waits for them, and re-layouts  71.2 us (7%)
  between operations  18 us (2%)
  matrix products  17.5 us (2%)
    psum x1, waiting for transfers between devices, per_device(): summed = lax.psum(partial_weight, ('member', 'space'))  449 us
    scatter-add x1, other arithmetic, per_device(): jax.ops.segment_sum(edge_terms, flat_index, num_segments=3 * nodes_dev)  211 us
    psum x1, blocking collectives, per_device(): lax.psum((target_sums, pair_sums, cell_count), 'space')  113 us
    all_gather x1, waiting for transfers between devices, per_device(): lax.all_gather(fields, 'member', axis=0, tiled=True).astype(jnp.float32)  67.4 us
    gather x1, local copies, waits for them, and re-layouts, per_device(): jnp.take(extended, local_index.reshape(-1), axis=1)  41.8 us
    reduce_sum x16, other arithmetic, against(): return jnp.sum(valid_rows * spread * spread, axis=(1, 2))  33.9 us
  transfers between devices with their start and end apart: 6, of which 3 were waited for; matrix products, arithmetic and copies ran while one was open for 1% of the time, Pallas kernels for 0%

commit v1 on v0

--- a/solution.py
+++ b/solution.py
@@ -91,7 +91,7 @@
     partial_weight = jnp.einsum(
         "mvg,mgd->vd", grad_fields, hidden, preferred_element_type=jnp.float32
     )
-    summed = lax.psum(partial_weight, ("member", "space"))
+    summed = lax.psum(lax.psum(partial_weight, "space"), "member")
     column_count = latent_width // lax.axis_size("space")
     grad_w_out = lax.dynamic_slice_in_dim(summed, band_index * column_count, column_count, 1)
     back = jnp.einsum("vd,mvg->mgd", w_out, grad_fields, preferred_element_type=jnp.float32)

time: 1040 us -> 855 us (0.82)
  the two profiles are of different devices: /device:TPU:4 before, /device:TPU:32 now
where the time goes in v1:
time: 855 us; the launch traced here: 851 us
  waiting for transfers between devices  342 us (40%)
  other arithmetic  286 us (33%)
  blocking collectives  107 us (13%)
  local copies, waits for them, and re-layouts  70.5 us (8%)
  between operations  17.8 us (2%)
  matrix products  15.7 us (2%)
  starting transfers between devices  11.6 us (1%)
    psum x2, waiting for transfers between devices, per_device(): summed = lax.psum(lax.psum(partial_weight, 'space'), 'member')  272 us
    scatter-add x1, other arithmetic, per_device(): jax.ops.segment_sum(edge_terms, flat_index, num_segments=3 * nodes_dev)  212 us
    psum x1, blocking collectives, per_device(): lax.psum((target_sums, pair_sums, cell_count), 'space')  107 us
    all_gather x1, waiting for transfers between devices, per_device(): lax.all_gather(fields, 'member', axis=0, tiled=True).astype(jnp.float32)  67 us
    gather x1, local copies, waits for them, and re-layouts, per_device(): jnp.take(extended, local_index.reshape(-1), axis=1)  41.8 us
    reduce_sum x16, other arithmetic, against(): return jnp.sum(valid_rows * spread * spread, axis=(1, 2))  33.9 us
  transfers between devices with their start and end apart: 7, of which 5 were waited for; matrix products, arithmetic and copies ran while one was open for 29% of the time, Pallas kernels for 0%

profile of v1, /device:TPU:32, one launch (start us, length us, event | category | flops | bytes accessed | tf_op | source)
XLA Modules:
  0.0 850.9 jit_solution(10407170358902310390)
XLA Ops:
  10.5 3.6 collective-permute-start.1
  20.1 41.8 %gather_fusion = bf16[1536,2,1024]{2,1,0:T(2,128)(2,1)} fusion(bf16[2,192,1024]{2,0,1:T(2,128)(2,1)S(1)} %pad_maximum_fusion, s32[2048]{0:T(1024)S(1)} %pad_clamp_fusion), kind=kCustom, calls=%fused_computation | custom fusion | bytes 12589056 | tf_op jit(solution)/shard_map/jit(_take)/gather | solution.py:66
  61.9 6.4 copy_select_fusion
  68.3 4.7 multiply_convert_fusion.1
  77.4 67.0 %all-gather.2.cloned.1.call-done = bf16[16,69,512]{2,1,0:T(8,128)(2,1)} async-done(((bf16[2,69,512]{2,1,0:T(8,128)(2,1)}), bf16[16,69,512]{2,1,0:T(8,128)(2,1)}) %all-gather.2.cloned.1.call-update) | async-done | bytes 1130512 | tf_op jit(solution)/shard_map/all_gather | solution.py:81
  144.4 3.0 convert_element_type.76
  147.4 59.9 %while.11 = (s32[]{:T(128)}, f32[16,16]{1,0:T(8,128)S(1)}, f32[16,69,512]{2,1,0:T(8,128)}, s32[]{:T(128)}, s32[]{:T(128)}, /*index=5*/s32[]{:T(128)}) while((s32[]{:T(128)}, f32[16,16]{1,0:T(8,128)S(1)}, f32[16,69,512]{2,1,0:T(8,128)}, s32[]{:T(128)}, s32[]{:T(128)}, /*index=5*/s32[]{:T(128)}) %tuple.38), condition=%wide.region_7.8_spmd.clone, body=%wide.region_5.7_spmd.clone.sunk | while | flops 2262002 | bytes 2689297 | solution.py:36
  149.1 2.1 fusion.44
  152.9 2.1 fusion.44
  156.6 2.1 fusion.44
  160.3 2.1 fusion.44
  164.1 2.1 fusion.44
  167.8 2.1 fusion.44
  171.5 2.1 fusion.44
  175.3 2.1 fusion.44
  179.0 2.1 fusion.44
  208.8 107.4 %all-reduce = (f32[16]{0:T(128)S(1)}, f32[]{:T(128)}, f32[16,16]{1,0:T(8,128)S(1)}) all-reduce(f32[16]{0:T(128)S(1)} %fusion.7, f32[]{:T(128)} %fusion.30, f32[16,16]{1,0:T(8,128)S(1)} %get-tuple-element.25), channel_id=1, replica_groups=mesh['member'=8,'space'=64] {'space'}, use_global_device_ids=true, to_apply=%region_1.2 | all-reduce | flops 273 | bytes 2184 | tf_op jit(solution)/shard_map/psum | solution.py:83
  321.8 7.7 fusion.10
  329.5 5.4 copy.33
  334.9 10.1 %bitcast_multiply_fusion = f32[2,1536,1024]{2,0,1:T(2,128)} fusion(f32[1536]{0:T(1024)S(1)} %mul.143, f32[2,512,1024]{2,0,1:T(2,128)S(1)} %copy.33), kind=kLoop, calls=%fused_computation.8 | loop fusion | flops 3145728 | bytes 16783360 | tf_op jit(solution)/shard_map/mul | solution.py:101
  346.6 211.6 %scatter_fusion = f32[2,192,1024]{2,0,1:T(2,128)} fusion(f32[2,192,1024]{2,0,1:T(2,128)} %broadcast_in_dim.23, s32[1536]{0:T(1024)S(1)} %reshape.87, f32[1536,2,1024]{2,1,0:T(2,128)} %bitcast.66), kind=kCustom, calls=%fused_computation.1 | custom fusion | flops 3145728 | bytes 37754880 | tf_op jit(solution)/shard_map/vmap()/scatter-add | solution.py:106
  560.5 3.9 collective-permute-start.2
  566.3 177.0 %all-reduce.4.cloned.1.call-done = f32[69,1024]{0,1:T(8,128)} async-done(((f32[69,1024]{0,1:T(8,128)}), f32[69,1024]{0,1:T(8,128)}) %all-reduce.4.cloned.1.call-update) | async-done | bytes 282640 | tf_op jit(solution)/shard_map/psum | solution.py:94
  746.8 95.2 %all-reduce.6.cloned.1.call-done = f32[69,1024]{0,1:T(8,128)} async-done(((f32[69,1024]{0,1:T(8,128)}), f32[69,1024]{0,1:T(8,128)}) %all-reduce.6.cloned.1.call-update) | async-done | bytes 282640 | tf_op jit(solution)/shard_map/psum | solution.py:94
  (114 shorter events, 68.9 us)
Async XLA Ops:
  7.2 61.1 %copy-start = (bf16[1024,1024]{1,0:T(8,128)(2,1)S(1)}, bf16[1024,1024]{1,0:T(8,128)(2,1)}, u32[]{:S(2)}) copy-start(bf16[1024,1024]{1,0:T(8,128)(2,1)} %param.13) | copy-start | bytes 6291460
  7.2 137.2 %all-gather.2.cloned.1.call-start = ((), (), s32[]{:S(2)}) async-start(), calls=%async_computation | async-start | bytes 1327104 | tf_op jit(solution)/shard_map/all_gather | solution.py:81
  8.6 7.7 collective-permute-start
  10.5 7.5 collective-permute-start.1
  68.3 6.1 copy-start.7
  68.3 7.8 copy-start.9
  73.1 1.3 copy-start.2
  75.9 667.4 %all-reduce.4.cloned.1.call-start = ((), (), s32[]{:S(2)}) async-start(), calls=%async_computation.1 | async-start | bytes 1048576 | tf_op jit(solution)/shard_map/psum | solution.py:94
  147.4 59.9 %copy-start.1 = (bf16[16,69,512]{2,1,0:T(8,128)(2,1)S(1)}, bf16[16,69,512]{2,1,0:T(8,128)(2,1)}, u32[]{:S(2)}) copy-start(bf16[16,69,512]{2,1,0:T(8,128)(2,1)} %all-gather.2.cloned.1.call-done) | copy-start | bytes 3391492
  207.3 112.5 %copy-start.4 = (bf16[2,69,512]{2,1,0:T(8,128)(2,1)S(1)}, bf16[2,69,512]{2,1,0:T(8,128)(2,1)}, u32[]{:S(2)}) copy-start(bf16[2,69,512]{2,1,0:T(8,128)(2,1)} %fusion.16) | copy-start | bytes 423940
  316.9 2.9 copy-start.3
  316.9 2.9 copy-start.5
  318.7 3.0 copy-start.6
  318.8 3.0 copy-start.8
  321.7 520.3 %all-reduce.6.cloned.1.call-start = ((), (), s32[]{:S(2)}) async-start(), calls=%async_computation.2 | async-start | bytes 1048576 | tf_op jit(solution)/shard_map/psum | solution.py:94
  560.5 184.1 %collective-permute-start.2 = (bf16[2,64,1024]{2,0,1:T(2,128)(2,1)S(1)}, bf16[2,64,1024]{2,0,1:T(2,128)(2,1)S(1)}, u32[]{:S(2)}, u32[]{:S(2)}) collective-permute-start(bf16[2,64,1024]{2,0,1:T(2,128)(2,1)S(1)} %get-tuple-element.68), channel_id=1, source_target_pairs={{1,0},{2,1},{3,2},{4,3},{5,4},{6,5},{7,6},{8,7},{9,8},{10,9},{11,1... | collective-permute-start | bytes 786440 | tf_op jit(solution)/shard_map/ppermute | solution.py:25
  564.4 180.3 %collective-permute-start.3 = (bf16[2,64,1024]{2,0,1:T(2,128)(2,1)S(1)}, bf16[2,64,1024]{2,0,1:T(2,128)(2,1)S(1)}, u32[]{:S(2)}, u32[]{:S(2)}) collective-permute-start(bf16[2,64,1024]{2,0,1:T(2,128)(2,1)S(1)} %get-tuple-element.69), channel_id=1, source_target_pairs={{0,1},{1,2},{2,3},{3,4},{4,5},{5,6},{6,7},{7,8},{8,9},{9,10},{10,1... | collective-permute-start | bytes 786440 | tf_op jit(solution)/shard_map/ppermute | solution.py:25
Sparse Core Ops, SparseCore 0:
  76.0 68.3 all-gather.1
  321.8 421.4 all-reduce.3
  746.5 95.4 all-reduce.5
